TPU v7x, 32 devices: a whole 2x2x4 slice. The times are simulated.
32 devices in a mesh: req: 4 (over y, x), mlp: 8 (over z, core).
Axes of the slice: x: 2, y: 2, z: 4, core: 2. Of those that a mesh axis runs over, the one named last changes fastest.
Arguments:
- hidden: bfloat16 [8, 5, 4096], P('req', None, 'mlp'), may hold values from -6 to 6
- attn_gain: float32 [4096], P('mlp'), may hold values from 0.1 to 1.9
- w_qkv: bfloat16 [4096, 6144], P('mlp'), may hold values from -0.09375 to 0.09375
- w_out: bfloat16 [4096, 4096], P(None, 'mlp'), may hold values from -0.09375 to 0.09375
- mlp_gain: float32 [4096], replicated, may hold values from 0.1 to 1.9
- w_gate: bfloat16 [4096, 14336], P(None, ('req', 'mlp')), may hold values from -0.09375 to 0.09375
- w_up: bfloat16 [4096, 14336], P(None, ('req', 'mlp')), may hold values from -0.09375 to 0.09375
- w_down: bfloat16 [14336, 4096], P(('req', 'mlp')), may hold values from -0.09375 to 0.09375
- kv_cache: bfloat16 [8, 1024, 2048], P('req', 'mlp')
- lengths: int32 [8], P('req'), may hold values from 1 to 1024, as said below
- mig_slot: int32 [4], replicated, may hold values from 0 to 1, as said below
- mig_dest: int32 [4], replicated, may hold values from 0 to 3, each once
Outputs:
- layer_out: bfloat16 [8, 5, 4096], P('req', None, 'mlp')
- moved_cache: bfloat16 [4, 128, 2048], P('req', 'mlp')
Inputs may be any that keep to these rules, and one draw needn't show every extreme that they name: `mig_slot`: the slot of each group that its leaving request vacates and the arriving one takes. `mig_dest`: A permutation of the groups: every group receives exactly one request. `lengths`: in slot g * 2 + mig_slot[g] the length is at most 128, reached in some group; some slot has exactly 1024.
All inputs are finite; a program needn't handle non-finite values.
Results may differ from a plain program's by a relative error of at most 0.012.
The roundings to bfloat16 on the way count: a program that leaves them out, or rounds other values in their place, can miss the bound.
Values may be sent and summed in bfloat16 or wider, within the bound.
A program may use at most 128 MiB of HBM per device.

v0:
```python
import jax
import jax.numpy as jnp
from jax import lax
from jax.sharding import PartitionSpec as P

D = 4096
HEADS = 32
KVH = 8
HD = 128
MIG_ROWS = 16
EPSILON = 1e-05
ROPE_BASE = 500000.0
NEG_FILL = -1e30


def merged_2(shard, axis, combine):
    everything = jax.tree.map(lambda part: lax.all_gather(part, axis), shard)
    initial = jax.tree.map(lambda part: part[0], everything)

    def lap(k, so_far):
        return combine(so_far, jax.tree.map(lambda part: part[k], everything))

    return lax.fori_loop(1, lax.axis_size(axis), lap, initial)


def rotate(vectors, positions):
    half_dim = vectors.shape[-1] // 2
    frequency = ROPE_BASE ** (-(jnp.arange(half_dim).astype(jnp.float32) / half_dim))
    angles = positions.astype(jnp.float32)[..., None, None] * frequency
    cos_part = jnp.cos(angles)
    sin_part = jnp.sin(angles)
    leading = vectors[..., :half_dim]
    trailing = vectors[..., half_dim:]
    return jnp.concatenate(
        [leading * cos_part - trailing * sin_part, trailing * cos_part + leading * sin_part],
        axis=-1,
    )


def combine(former, latter):
    former_max, former_sum, former_acc = former
    latter_max, latter_sum, latter_acc = latter
    highest = jnp.maximum(former_max, latter_max)
    former_rate = jnp.exp(former_max - highest)
    latter_rate = jnp.exp(latter_max - highest)
    return (
        highest,
        former_sum * former_rate + latter_sum * latter_rate,
        former_acc * former_rate[..., None] + latter_acc * latter_rate[..., None],
    )


def softmax_part(scores, usable, values, pattern):
    highest = jnp.max(jnp.where(usable, scores, NEG_FILL), axis=-1)
    weights = jnp.where(usable, jnp.exp(scores - highest[..., None]), 0.0)
    mixture = jnp.einsum(
        pattern, weights.astype(jnp.bfloat16), values, preferred_element_type=jnp.float32
    )
    return (highest, jnp.sum(weights, axis=-1), mixture)


def body(
    hidden,
    attn_gain,
    w_qkv,
    w_out,
    mlp_gain,
    w_gate,
    w_up,
    w_down,
    kv_cache,
    lengths,
    mig_slot,
    mig_dest,
):
    group_count = lax.axis_size("req")
    block_count = lax.axis_size("mlp")
    group_id = lax.axis_index("req")
    block_id = lax.axis_index("mlp")
    slot_count, spec_len, width_dev = hidden.shape
    ctx_dev = kv_cache.shape[1]
    kv_width = kv_cache.shape[2] // 2
    zero_index = jnp.zeros((), jnp.int32)
    own_slot = mig_slot[group_id]
    target = mig_dest[group_id]
    source = jnp.sum(jnp.where(mig_dest == group_id, jnp.arange(group_count, dtype=jnp.int32), 0))
    leaving = lax.dynamic_index_in_dim(kv_cache, own_slot, 0, keepdims=False)[:MIG_ROWS]
    outgoing = jnp.zeros((group_count,) + leaving.shape, leaving.dtype)
    outgoing = lax.dynamic_update_slice(outgoing, leaving[None], (target, zero_index, zero_index))
    incoming = lax.all_to_all(outgoing, "req", split_axis=0, concat_axis=0, tiled=True)
    arrived = lax.dynamic_index_in_dim(incoming, source, 0, keepdims=False)
    live_cache = lax.dynamic_update_slice(
        kv_cache, arrived[None], (own_slot, zero_index, zero_index)
    )
    widened = hidden.astype(jnp.float32)
    square_part = jnp.sum(widened * widened, axis=-1)
    scaled = (widened * attn_gain).astype(jnp.bfloat16)
    projected = jnp.einsum("rsd,de->rse", scaled, w_qkv, preferred_element_type=jnp.float32)
    square_sum, projected = lax.psum((square_part, projected), "mlp")
    projected = projected * lax.rsqrt(square_sum / D + EPSILON)[..., None]
    positions = lengths[:, None] + jnp.arange(spec_len, dtype=jnp.int32)[None, :]
    query_width = HEADS * HD
    queries = rotate(
        projected[..., :query_width].reshape(slot_count, spec_len, HEADS, HD), positions
    ).astype(jnp.bfloat16)
    new_keys = rotate(
        projected[..., query_width : query_width + kv_width].reshape(slot_count, spec_len, KVH, HD),
        positions,
    ).astype(jnp.bfloat16)
    new_values = (
        projected[..., query_width + kv_width :]
        .reshape(slot_count, spec_len, KVH, HD)
        .astype(jnp.bfloat16)
    )
    grouped = queries.reshape(slot_count, spec_len, KVH, HEADS // KVH, HD)
    score_scale = HD ** (-0.5)
    cached_keys = live_cache[..., :kv_width].reshape(slot_count, ctx_dev, KVH, HD)
    cached_values = live_cache[..., kv_width:].reshape(slot_count, ctx_dev, KVH, HD)
    scores = (
        jnp.einsum("rsgqd,rcgd->rgsqc", grouped, cached_keys, preferred_element_type=jnp.float32)
        * score_scale
    )
    stored = jnp.arange(ctx_dev, dtype=jnp.int32) * block_count + block_id
    usable = (stored[None, :] < lengths[:, None])[:, None, None, None, :]
    block_part = softmax_part(scores, usable, cached_values, "rgsqc,rcgd->rgsqd")
    merged = merged_2(block_part, "mlp", combine)
    own_scores = (
        jnp.einsum("rsgqd,rtgd->rgsqt", grouped, new_keys, preferred_element_type=jnp.float32)
        * score_scale
    )
    causal = (jnp.arange(spec_len)[:, None] >= jnp.arange(spec_len)[None, :])[
        None, None, :, None, :
    ]
    own_part = softmax_part(own_scores, causal, new_values, "rgsqt,rtgd->rgsqd")
    highest, summed, mixture = combine(merged, own_part)
    attended = (
        (mixture / summed[..., None])
        .transpose(0, 2, 1, 3, 4)
        .reshape(slot_count, spec_len, query_width)
        .astype(jnp.bfloat16)
    )
    residual = (
        widened + jnp.einsum("rse,ed->rsd", attended, w_out, preferred_element_type=jnp.float32)
    ).astype(jnp.bfloat16)
    gathered = lax.all_gather(residual[None], ("req", "mlp"), axis=0, tiled=True)
    token_group = slot_count * spec_len
    gathered = gathered.reshape(group_count, block_count, token_group, width_dev)
    widened_rows = gathered.astype(jnp.float32)
    inverse = lax.rsqrt(jnp.sum(widened_rows * widened_rows, axis=(1, 3)) / D + EPSILON)
    scaled_rows = (widened_rows * mlp_gain.reshape(block_count, 1, width_dev)).astype(jnp.bfloat16)
    hidden_dev = w_gate.shape[1]
    gate_proj = (
        jnp.einsum(
            "rmtc,mcf->rtf",
            scaled_rows,
            w_gate.reshape(block_count, width_dev, hidden_dev),
            preferred_element_type=jnp.float32,
        )
        * inverse[..., None]
    )
    up_proj = (
        jnp.einsum(
            "rmtc,mcf->rtf",
            scaled_rows,
            w_up.reshape(block_count, width_dev, hidden_dev),
            preferred_element_type=jnp.float32,
        )
        * inverse[..., None]
    )
    activated = (jax.nn.silu(gate_proj) * up_proj).astype(jnp.bfloat16)
    down_cols = w_down.reshape(hidden_dev, block_count, width_dev)
    block_index = jnp.arange(
        lax.axis_size(("req", "mlp")) * token_group // token_group, dtype=jnp.int32
    )
    row_sel = jnp.take(activated, block_index // block_count, axis=0)
    col_sel = jnp.take(down_cols, block_index % block_count, axis=1)
    product = jnp.einsum("ktf,fkc->ktc", row_sel, col_sel, preferred_element_type=jnp.float32)
    added = lax.psum_scatter(
        product.reshape(lax.axis_size(("req", "mlp")) * token_group, width_dev),
        ("req", "mlp"),
        scatter_dimension=0,
        tiled=True,
    )
    layer_out = (
        residual.astype(jnp.float32) + added.reshape(slot_count, spec_len, width_dev)
    ).astype(jnp.bfloat16)
    return (layer_out, arrived[None])


def solution(mesh):
    placed = (
        P("req", None, "mlp"),
        P("mlp"),
        P("mlp", None),
        P(None, "mlp"),
        P(),
        P(None, ("req", "mlp")),
        P(None, ("req", "mlp")),
        P(("req", "mlp"), None),
        P("req", "mlp", None),
        P("req"),
        P(),
        P(),
    )
    return jax.shard_map(
        body,
        mesh=mesh,
        in_specs=placed,
        out_specs=(P("req", None, "mlp"), P("req", "mlp", None)),
        check_vma=False,
    )
```

profile of v0, /device:TPU:0, one launch (start us, length us, event | category | flops | bytes accessed | tf_op | source)
XLA Modules:
  0.0 325.4 jit_solution(10649896896473231463)
XLA Ops:
  7.3 4.6 %fusion.9 = f32[2,5,6144]{2,1,0:T(8,128)} fusion(bf16[512,6144]{1,0:T(8,128)(2,1)} %param.16, bf16[2,5,512]{2,0,1:T(2,128)(2,1)} %param.14, f32[512]{0:T(512)} %param.15), kind=kOutput, calls=%fused_computation.17 | convolution fusion | flops 62929920 | bytes 6549504 | tf_op jit(solution)/shard_map/rsd,de->rse/dot_general | solution.py:98
  11.9 0.6 dynamic_slice.46
  13.8 0.6 dynamic_slice.44
  17.0 0.7 broadcast_in_dim.99
  17.7 0.6 dynamic-slice_dynamic-update-slice_fusion
  18.4 5.2 %all-to-all-start = ((bf16[4,16,2048]{2,1,0:T(8,128)(2,1)}), bf16[4,16,2048]{2,1,0:T(8,128)(2,1)S(1)}, u32[]{:S(2)}, u32[]{:S(2)}) async-start(bf16[4,16,2048]{2,1,0:T(8,128)(2,1)} %dynamic-slice_dynamic-update-slice_fusion), calls=%async_computation | async-start | bytes 524288 | tf_op jit(solution)/shard_map/all_to_all | solution.py:90
  23.6 0.7 copy.134
  24.3 0.6 fusion.56
  26.2 16.4 %psum.15 = f32[2,5]{1,0:T(2,128)S(1)} all-reduce(f32[2,5]{1,0:T(2,128)S(1)} %fusion.47), channel_id=1, replica_groups=mesh['req'=4,'mlp'=8] {'mlp'}, use_global_device_ids=true, to_apply=%region_2.3 | all-reduce | flops 10 | bytes 80 | tf_op jit(solution)/shard_map/psum | solution.py:99
  43.6 26.7 %all-reduce.4.cloned.1.call-done = f32[2,5,6144]{2,1,0:T(8,128)} async-done(((f32[2,5,6144]{2,1,0:T(8,128)}), f32[2,5,6144]{2,1,0:T(8,128)}) %all-reduce.4.cloned.1.call-update) | async-done | bytes 245776 | tf_op jit(solution)/shard_map/psum | solution.py:99
  70.3 1.1 broadcast_multiply_fusion
  71.9 0.3 copy.184
  72.1 2.0 dynamic_update_slice.7
  74.2 0.4 select_reduce_fusion
  74.6 0.4 fusion.37
  75.0 0.8 copy.139
  75.9 4.2 %copy.227 = bf16[56,8,8,512]{3,2,0,1:T(8,128)(2,1)} copy(bf16[56,8,8,512]{3,2,1,0:T(8,128)(2,1)} %bitcast.134) | data formatting | bytes 7340032 | tf_op jit(solution)/shard_map/reshape | solution.py:171
  80.1 9.3 %gather_fusion.1 = bf16[32,448,512]{2,1,0:T(8,128)(2,1)} fusion(bf16[448,8,512]{2,0,1:T(8,128)(2,1)} %bitcast.133, s32[1024]{0:T(1024)S(1)} %pad_clamp_fusion), kind=kCustom, calls=%fused_computation.1 | custom fusion | bytes 29360256 | tf_op jit(solution)/shard_map/jit(_take)/gather | solution.py:176
  89.6 0.7 fusion.48
  90.3 0.4 copy.145
  91.1 0.4 copy.152
  91.7 14.0 %all-gather = f32[16,8,5,4]{1,3,2,0:T(4,128)S(1)} all-gather(f32[2,8,5,4]{1,3,2,0:T(4,128)S(1)} %copy.136), channel_id=2, replica_groups=mesh['req'=4,'mlp'=8] {'mlp'}, dimensions={0}, use_global_device_ids=true | all-gather | bytes 11520 | tf_op jit(solution)/shard_map/all_gather | solution.py:17
  105.7 0.3 fusion.36
  106.2 14.0 %all-gather.1 = f32[16,8,5,4]{1,3,2,0:T(4,128)S(1)} all-gather(f32[2,8,5,4]{1,3,2,0:T(4,128)S(1)} %copy.137), channel_id=3, replica_groups=mesh['req'=4,'mlp'=8] {'mlp'}, dimensions={0}, use_global_device_ids=true | all-gather | bytes 11520 | tf_op jit(solution)/shard_map/all_gather | solution.py:17
  120.2 0.9 slice.68
  121.2 12.6 %while.19 = (s32[]{:T(128)}, f32[2,8,5,4]{1,3,2,0:T(4,128)S(1)}, f32[2,8,5,4]{1,3,2,0:T(4,128)S(1)}, f32[2,8,5,4,128]{4,3,2,1,0:T(4,128)S(1)}, f32[8,2,8,5,4]{2,...) while((s32[]{:T(128)}, f32[2,8,5,4]{1,3,2,0:T(4,128)S(1)}, ...), condition=%wide.region_7.8_spmd, body=%wide.region_6.7_spmd.sunk | while | flops 124805 | bytes 837271 | solution.py:23
  121.2 0.9 constant_dynamic-slice_fusion.4
  122.2 0.1 copy.232
  122.3 0.1 copy.233
  122.4 0.5 fusion.73
  123.0 0.9 constant_dynamic-slice_fusion.4
  124.0 0.1 copy.232
  124.1 0.1 copy.233
  124.2 0.5 fusion.73
  124.8 0.9 constant_dynamic-slice_fusion.4
  125.8 0.1 copy.232
  125.9 0.1 copy.233
  126.0 0.5 fusion.73
  126.6 0.9 constant_dynamic-slice_fusion.4
  127.6 0.1 copy.232
  127.7 0.1 copy.233
  127.8 0.5 fusion.73
  128.4 0.9 constant_dynamic-slice_fusion.4
  129.4 0.1 copy.232
  129.5 0.1 copy.233
  129.6 0.5 fusion.73
  130.2 0.9 constant_dynamic-slice_fusion.4
  131.2 0.1 copy.232
  131.4 0.5 fusion.73
  132.0 0.9 constant_dynamic-slice_fusion.4
  133.0 0.1 copy.232
  133.2 0.5 fusion.73
  134.1 0.3 fusion.19
  134.4 2.9 fusion.29
  137.3 41.9 %all-gather.3 = bf16[64,5,512]{2,1,0:T(8,128)(2,1)S(1)} all-gather(bf16[2,5,512]{2,1,0:T(8,128)(2,1)S(1)} %fusion.29), channel_id=5, replica_groups=mesh['req'=4,'mlp'=8] {'req','mlp'}, dimensions={0}, use_global_device_ids=true | all-gather | bytes 337920 | tf_op jit(solution)/shard_map/all_gather | solution.py:145
  179.3 0.2 multiply_reduce_fusion
  179.6 3.4 %fusion.24 = f32[4,10,448]{2,1,0:T(8,128)S(1)} fusion(bf16[56,8,8,512]{3,2,1,0:T(8,128)(2,1)} %bitcast.153, f32[4,8,10,512]{3,2,1,0:T(8,128)S(1)} %reshape.225, f32[8,512]{1,0:T(8,128)S(1)} %mul.286, f32[4,10]{1,0:T(4,128)S(1)} %add_rsqrt_fusion), kind=kOutput, calls=%fused_computation.37 | convolution fusion | flops 147146240 | bytes 4413600 | tf_op jit(solution)/shard_map/rmtc,mcf->rtf/dot_general | solution.py:153
  183.0 1.2 fusion.25
  184.2 0.6 gather_fusion
  184.8 6.5 %fusion.4 = f32[32,10,512]{2,1,0:T(8,128)S(1)} fusion(bf16[32,448,512]{2,1,0:T(8,128)(2,1)} %gather_fusion.1, pred[32]{0:T(512)(128)(4,1)S(1)} %get-tuple-element.263, bf16[32,10,448]{2,1,0:T(8,128)(2,1)S(1)} %gather_fusion, pred[32]{0:T(512)(128)(4,1)S(1)} %get-tuple-element.264), kind=kOutput, calls=%fused_computation.12 | convolution fusion | flops 154284032 | bytes 15622208 | tf_op jit(solution)/shard_map/ktf,fkc->ktc/dot_general | solution.py:177
  191.2 0.9 reshape.223
  192.2 125.3 %all-reduce.6.cloned.1.call-done = f32[320,512]{1,0:T(8,128)} async-done(((f32[320,512]{1,0:T(8,128)}), f32[320,512]{1,0:T(8,128)}) %all-reduce.6.cloned.1.call-update) | async-done | bytes 655376
  317.5 0.8 constant_dynamic-slice_fusion.2
  318.3 0.6 copy.159
  (79 shorter events, 3.1 us)
Async XLA Ops:
  7.2 16.4 %copy-start.2 = (bf16[2,5,512]{2,0,1:T(2,128)(2,1)S(1)}, bf16[2,5,512]{2,0,1:T(2,128)(2,1)}, u32[]{:S(2)}) copy-start(bf16[2,5,512]{2,0,1:T(2,128)(2,1)} %param.14) | copy-start | bytes 30724
  7.2 4.7 %copy-start.6 = (s32[4]{0:T(128)S(1)}, s32[4]{0:T(128)}, u32[]{:S(2)}) copy-start(s32[4]{0:T(128)} %param.25) | copy-start | bytes 52
  7.2 6.6 %copy-start.5 = (s32[4]{0:T(128)S(1)}, s32[4]{0:T(128)}, u32[]{:S(2)}) copy-start(s32[4]{0:T(128)} %param.24) | copy-start | bytes 52
  7.2 10.5 %copy-start = (bf16[2,128,2048]{2,1,0:T(8,128)(2,1)S(1)}, bf16[2,128,2048]{2,1,0:T(8,128)(2,1)}, u32[]{:S(2)}) copy-start(bf16[2,128,2048]{2,1,0:T(8,128)(2,1)} %param.22) | copy-start | bytes 3145732
  7.2 35.4 %copy-start.7 = (s32[2]{0:T(128)S(1)}, s32[2]{0:T(128)}, u32[]{:S(2)}) copy-start(s32[2]{0:T(128)} %param.23) | copy-start | bytes 28
  7.2 63.1 %all-reduce.4.cloned.1.call-start = ((), (), s32[]{:S(2)}) async-start(), calls=%async_computation.1 | async-start | bytes 786432 | tf_op jit(solution)/shard_map/psum | solution.py:99
  18.4 53.5 %all-to-all-start = ((bf16[4,16,2048]{2,1,0:T(8,128)(2,1)}), bf16[4,16,2048]{2,1,0:T(8,128)(2,1)S(1)}, u32[]{:S(2)}, u32[]{:S(2)}) async-start(bf16[4,16,2048]{2,1,0:T(8,128)(2,1)} %dynamic-slice_dynamic-update-slice_fusion), calls=%async_computation | async-start | bytes 524288 | tf_op jit(solution)/shard_map/all_to_all | solution.py:90
  23.5 96.7 %all-gather.6.cloned.1.call-start = ((), (), s32[]{:S(2)}) async-start(), calls=%async_computation.2 | async-start | bytes 1474560 | tf_op jit(solution)/shard_map/all_gather | solution.py:17
  71.9 8.2 %copy-start.1 = (bf16[1,16,2048]{2,1,0:T(8,128)(2,1)}, bf16[1,16,2048]{2,1,0:T(8,128)(2,1)S(1)}, u32[]{:S(2)}) copy-start(bf16[1,16,2048]{2,1,0:T(8,128)(2,1)S(1)} %constant_dynamic-slice_fusion.1) | copy-start | bytes 196612
  75.0 5.0 %copy-start.3 = (f32[4096]{0:T(1024)S(1)}, f32[4096]{0:T(1024)}, u32[]{:S(2)}) copy-start(f32[4096]{0:T(1024)} %param.18) | copy-start | bytes 49156
  75.9 241.6 %all-reduce.6.cloned.1.call-start = ((), (), s32[]{:S(2)}) async-start(), calls=%async_computation.3 | async-start | bytes 1310720
  179.6 3.4 %copy-start.4 = (bf16[4096,448]{0,1:T(8,128)(2,1)S(1)}, bf16[4096,448]{0,1:T(8,128)(2,1)}, u32[]{:S(2)}) copy-start(bf16[4096,448]{0,1:T(8,128)(2,1)} %param.20) | copy-start | bytes 11010052
Sparse Core Ops, SparseCore 0:
  12.0 58.2 all-reduce.3
  76.0 23.0 all-gather.5
  192.3 125.1 all-reduce.5
where the time goes:
time: 326 us; the launch traced here: 325 us
  waiting for transfers between devices  152 us (47%)
  blocking collectives  86.3 us (26%)
  local copies, waits for them, and re-layouts  34.3 us (11%)
  matrix products  20.4 us (6%)
  between operations  19.9 us (6%)
  other arithmetic  7.03 us (2%)
  starting transfers between devices  5.26 us (2%)
    unnamed x4, waiting for transfers between devices  125 us
    all_gather x1, blocking collectives, body(): lax.all_gather(residual[None], ('req', 'mlp'), axis=0, tiled=True)  41.9 us
    all_gather x2, blocking collectives, merged_2(): everything = jax.tree.map(lambda part: lax.all_gather(part, axis), shard)  28 us
    psum x1, waiting for transfers between devices, body(): square_sum, projected = lax.psum((square_part, projected), 'mlp')  26.7 us
    psum x1, blocking collectives, body(): square_sum, projected = lax.psum((square_part, projected), 'mlp')  16.4 us
    gather x1, local copies, waits for them, and re-layouts, body(): col_sel = jnp.take(down_cols, block_index % block_count, axis=1)  9.3 us
    dynamic_slice x7, local copies, waits for them, and re-layouts, lap(): return combine(so_far, jax.tree.map(lambda part: part[k], everything))  6.53 us
  transfers between devices with their start and end apart: 4, of which 2 were waited for; matrix products, arithmetic and copies ran while one was open for 7% of the time, Pallas kernels for 0%

commit v1 on v0

--- a/solution.py
+++ b/solution.py
@@ -11,6 +11,18 @@
 EPSILON = 1e-05
 ROPE_BASE = 500000.0
 NEG_FILL = -1e30
+
+
+def gather_by_bits(value, axis, dim):
+    ways, here, hop = (lax.axis_size(axis), lax.axis_index(axis), value.shape[dim])
+    line, have = (value, 1)
+    while have < ways:
+        line = jnp.concatenate(
+            [line, lax.ppermute(line, axis, [(d, (d - have) % ways) for d in range(ways)])],
+            axis=dim,
+        )
+        have = 2 * have
+    return jnp.roll(line, here * hop, axis=dim)
 
 
 def merged_2(shard, axis, combine):
@@ -142,7 +154,7 @@
     residual = (
         widened + jnp.einsum("rse,ed->rsd", attended, w_out, preferred_element_type=jnp.float32)
     ).astype(jnp.bfloat16)
-    gathered = lax.all_gather(residual[None], ("req", "mlp"), axis=0, tiled=True)
+    gathered = gather_by_bits(residual[None], ("req", "mlp"), 0)
     token_group = slot_count * spec_len
     gathered = gathered.reshape(group_count, block_count, token_group, width_dev)
     widened_rows = gathered.astype(jnp.float32)

time: 326 us -> 313 us (0.960)
  blocking collectives: 86.3 us -> 45 us
  waiting for transfers between devices: 152 us -> 173 us
  starting transfers between devices: 5.26 us -> 11.1 us
    all_gather x1 -> x0, blocking collectives: 41.9 us -> none  [body(): lax.all_gather(residual[None], ('req', 'mlp'), axis=0, tiled=True)]
    ppermute x0 -> x5, waiting for transfers between devices: none -> 14.6 us  [gather_by_bits(): lax.ppermute(line, axis, [(d, (d - have) % ways) for d in range(ways)])]
    unnamed x4, waiting for transfers between devices: 125 us -> 132 us
    ppermute x0 -> x5, starting transfers between devices: none -> 5.89 us  [gather_by_bits(): lax.ppermute(line, axis, [(d, (d - have) % ways) for d in range(ways)])]
  transfers between devices with their start and end apart: 4 -> 9, of which waited for: 2 -> 6; matrix products, arithmetic and copies ran while one was open for 7% -> 7% of each run, Pallas kernels for 0% -> 0%
where the time goes in v1:
time: 313 us; the launch traced here: 312 us
  waiting for transfers between devices  173 us (55%)
  blocking collectives  45 us (14%)
  local copies, waits for them, and re-layouts  34.7 us (11%)
  matrix products  20.4 us (7%)
  between operations  20 us (6%)
  starting transfers between devices  11.1 us (4%)
  other arithmetic  7.39 us (2%)
    unnamed x4, waiting for transfers between devices  132 us
    all_gather x2, blocking collectives, merged_2(): everything = jax.tree.map(lambda part: lax.all_gather(part, axis), shard)  28.6 us
    psum x1, waiting for transfers between devices, body(): square_sum, projected = lax.psum((square_part, projected), 'mlp')  26.7 us
    psum x1, blocking collectives, body(): square_sum, projected = lax.psum((square_part, projected), 'mlp')  16.4 us
    ppermute x5, waiting for transfers between devices, gather_by_bits(): lax.ppermute(line, axis, [(d, (d - have) % ways) for d in range(ways)])  14.6 us
    gather x1, local copies, waits for them, and re-layouts, body(): col_sel = jnp.take(down_cols, block_index % block_count, axis=1)  9.14 us
    dynamic_slice x7, local copies, waits for them, and re-layouts, lap(): return combine(so_far, jax.tree.map(lambda part: part[k], everything))  6.53 us
    dot_general x1, matrix products, body(): jnp.einsum('ktf,fkc->ktc', row_sel, col_sel, preferred_element_type=jnp.f...  6.45 us
  transfers between devices with their start and end apart: 9, of which 6 were waited for; matrix products, arithmetic and copies ran while one was open for 7% of the time, Pallas kernels for 0%

profile of v1, /device:TPU:0, one launch (start us, length us, event | category | flops | bytes accessed | tf_op | source)
XLA Modules:
  0.0 311.8 jit_solution(6770497114858041925)
XLA Ops:
  7.3 4.6 %fusion.9 = f32[2,5,6144]{2,1,0:T(8,128)} fusion(bf16[512,6144]{1,0:T(8,128)(2,1)} %param.16, bf16[2,5,512]{2,0,1:T(2,128)(2,1)} %param.14, f32[512]{0:T(512)} %param.15), kind=kOutput, calls=%fused_computation.17 | convolution fusion | flops 62929920 | bytes 6549504 | tf_op jit(solution)/shard_map/rsd,de->rse/dot_general | solution.py:110
  11.9 0.6 dynamic_slice.50
  13.8 0.6 dynamic_slice.48
  17.0 0.7 broadcast_in_dim.99
  17.7 0.6 dynamic-slice_dynamic-update-slice_fusion
  18.4 5.2 %all-to-all-start = ((bf16[4,16,2048]{2,1,0:T(8,128)(2,1)}), bf16[4,16,2048]{2,1,0:T(8,128)(2,1)S(1)}, u32[]{:S(2)}, u32[]{:S(2)}) async-start(bf16[4,16,2048]{2,1,0:T(8,128)(2,1)} %dynamic-slice_dynamic-update-slice_fusion), calls=%async_computation | async-start | bytes 524288 | tf_op jit(solution)/shard_map/all_to_all | solution.py:102
  23.6 0.7 copy.144
  24.3 0.6 fusion.58
  26.2 16.4 %psum.15 = f32[2,5]{1,0:T(2,128)S(1)} all-reduce(f32[2,5]{1,0:T(2,128)S(1)} %fusion.49), channel_id=1, replica_groups=mesh['req'=4,'mlp'=8] {'mlp'}, use_global_device_ids=true, to_apply=%region_2.3 | all-reduce | flops 10 | bytes 80 | tf_op jit(solution)/shard_map/psum | solution.py:111
  43.6 26.7 %all-reduce.4.cloned.1.call-done = f32[2,5,6144]{2,1,0:T(8,128)} async-done(((f32[2,5,6144]{2,1,0:T(8,128)}), f32[2,5,6144]{2,1,0:T(8,128)}) %all-reduce.4.cloned.1.call-update) | async-done | bytes 245776 | tf_op jit(solution)/shard_map/psum | solution.py:111
  70.3 1.1 broadcast_multiply_fusion
  71.9 0.3 copy.203
  72.2 2.0 dynamic_update_slice.7
  74.2 0.4 select_reduce_fusion
  74.7 0.4 fusion.39
  75.1 0.8 copy.149
  76.1 0.7 fusion.50
  76.8 0.4 copy.155
  77.6 0.4 copy.162
  78.2 14.6 %all-gather = f32[16,8,5,4]{1,3,2,0:T(4,128)S(1)} all-gather(f32[2,8,5,4]{1,3,2,0:T(4,128)S(1)} %copy.146), channel_id=2, replica_groups=mesh['req'=4,'mlp'=8] {'mlp'}, dimensions={0}, use_global_device_ids=true | all-gather | bytes 11520 | tf_op jit(solution)/shard_map/all_gather | solution.py:29
  92.8 0.3 fusion.38
  93.2 14.0 %all-gather.1 = f32[16,8,5,4]{1,3,2,0:T(4,128)S(1)} all-gather(f32[2,8,5,4]{1,3,2,0:T(4,128)S(1)} %copy.147), channel_id=3, replica_groups=mesh['req'=4,'mlp'=8] {'mlp'}, dimensions={0}, use_global_device_ids=true | all-gather | bytes 11520 | tf_op jit(solution)/shard_map/all_gather | solution.py:29
  107.3 0.9 slice.68
  108.3 12.6 %while.19 = (s32[]{:T(128)}, f32[2,8,5,4]{1,3,2,0:T(4,128)S(1)}, f32[2,8,5,4]{1,3,2,0:T(4,128)S(1)}, f32[2,8,5,4,128]{4,3,2,1,0:T(4,128)S(1)}, f32[8,2,8,5,4]{2,...) while((s32[]{:T(128)}, f32[2,8,5,4]{1,3,2,0:T(4,128)S(1)}, ...), condition=%wide.region_7.8_spmd, body=%wide.region_6.7_spmd.sunk | while | flops 124805 | bytes 837271 | solution.py:35
  108.3 0.9 constant_dynamic-slice_fusion.4
  109.3 0.1 copy.260
  109.5 0.5 fusion.75
  110.1 0.9 constant_dynamic-slice_fusion.4
  111.1 0.1 copy.260
  111.3 0.5 fusion.75
  111.9 0.9 constant_dynamic-slice_fusion.4
  112.9 0.1 copy.260
  113.1 0.5 fusion.75
  113.7 0.9 constant_dynamic-slice_fusion.4
  114.7 0.1 copy.260
  114.9 0.5 fusion.75
  115.5 0.9 constant_dynamic-slice_fusion.4
  116.7 0.5 fusion.75
  117.3 0.9 constant_dynamic-slice_fusion.4
  118.5 0.5 fusion.75
  119.1 0.9 constant_dynamic-slice_fusion.4
  120.3 0.5 fusion.75
  121.1 0.3 fusion.19
  121.5 2.9 constant_dynamic-update-slice_fusion.4
  124.4 3.1 collective-permute-start
  127.5 1.4 collective-permute-done
  128.9 0.8 collective-permute-start.1
  129.7 3.2 %collective-permute-done.1 = bf16[2,2,5,512]{3,2,1,0:T(8,128)(2,1)S(1)} collective-permute-done((bf16[2,2,5,512]{3,2,1,0:T(8,128)(2,1)S(1)}, bf16[2,2,5,512]{3,2,1,0:T(8,128)(2,1)S(1)}, u32[]{:S(2)}, u32[]{:S(2)}) %collective-permute-start.1) | collective-permute-done | bytes 20512 | tf_op jit(solution)/shard_map/ppermute | solution.py:21
  133.0 5.1 %collective-permute-done.2 = bf16[4,2,5,512]{3,2,1,0:T(8,128)(2,1)S(1)} collective-permute-done((bf16[4,2,5,512]{3,2,1,0:T(8,128)(2,1)S(1)}, bf16[4,2,5,512]{3,2,1,0:T(8,128)(2,1)S(1)}, u32[]{:S(2)}, u32[]{:S(2)}) %collective-permute-start.2) | collective-permute-done | bytes 40992 | tf_op jit(solution)/shard_map/ppermute | solution.py:21
  138.2 1.3 collective-permute-start.3
  139.5 4.9 %collective-permute-done.3 = bf16[8,2,5,512]{3,2,1,0:T(8,128)(2,1)S(1)} collective-permute-done((bf16[8,2,5,512]{3,2,1,0:T(8,128)(2,1)S(1)}, bf16[8,2,5,512]{3,2,1,0:T(8,128)(2,1)S(1)}, u32[]{:S(2)}, u32[]{:S(2)}) %collective-permute-start.3) | collective-permute-done | bytes 81952 | tf_op jit(solution)/shard_map/ppermute | solution.py:21
  144.4 0.6 collective-permute-start.4
  145.0 4.2 %copy.255 = bf16[56,8,8,512]{3,2,0,1:T(8,128)(2,1)} copy(bf16[56,8,8,512]{3,2,1,0:T(8,128)(2,1)} %bitcast.152) | data formatting | bytes 7340032 | tf_op jit(solution)/shard_map/reshape | solution.py:183
  149.2 9.1 %gather_fusion.1 = bf16[32,448,512]{2,1,0:T(8,128)(2,1)} fusion(bf16[448,8,512]{2,0,1:T(8,128)(2,1)} %bitcast.151, s32[1024]{0:T(1024)S(1)} %pad_clamp_fusion), kind=kCustom, calls=%fused_computation.1 | custom fusion | bytes 29360256 | tf_op jit(solution)/shard_map/jit(_take)/gather | solution.py:188
  158.6 0.2 multiply_reduce_fusion
  158.9 0.4 copy.166
  159.7 3.4 %fusion.24 = f32[4,10,448]{2,1,0:T(8,128)S(1)} fusion(bf16[56,8,8,512]{3,2,1,0:T(8,128)(2,1)} %bitcast.176, bf16[4,8,10,512]{3,1,0,2:T(8,128)(2,1)S(1)} %multiply_convert_fusion, f32[4,10]{1,0:T(4,128)S(1)} %add_rsqrt_fusion), kind=kOutput, calls=%fused_computation.37 | convolution fusion | flops 146818560 | bytes 4069536 | tf_op jit(solution)/shard_map/rmtc,mcf->rtf/dot_general | solution.py:165
  163.1 1.2 fusion.25
  164.3 0.6 gather_fusion
  164.9 6.4 %fusion.4 = f32[32,10,512]{2,1,0:T(8,128)S(1)} fusion(bf16[32,448,512]{2,1,0:T(8,128)(2,1)} %gather_fusion.1, pred[32]{0:T(512)(128)(4,1)S(1)} %get-tuple-element.274, bf16[32,10,448]{2,1,0:T(8,128)(2,1)S(1)} %gather_fusion, pred[32]{0:T(512)(128)(4,1)S(1)} %get-tuple-element.275), kind=kOutput, calls=%fused_computation.12 | convolution fusion | flops 154284032 | bytes 15622208 | tf_op jit(solution)/shard_map/ktf,fkc->ktc/dot_general | solution.py:189
  171.3 0.9 reshape.223
  172.3 131.5 %all-reduce.6.cloned.1.call-done = f32[320,512]{1,0:T(8,128)} async-done(((f32[320,512]{1,0:T(8,128)}), f32[320,512]{1,0:T(8,128)}) %all-reduce.6.cloned.1.call-update) | async-done | bytes 655376
  303.9 0.8 constant_dynamic-slice_fusion.2
  304.7 0.6 copy.174
  (105 shorter events, 4.8 us)
Async XLA Ops:
  7.2 16.4 %copy-start.2 = (bf16[2,5,512]{2,0,1:T(2,128)(2,1)S(1)}, bf16[2,5,512]{2,0,1:T(2,128)(2,1)}, u32[]{:S(2)}) copy-start(bf16[2,5,512]{2,0,1:T(2,128)(2,1)} %param.14) | copy-start | bytes 30724
  7.2 4.7 %copy-start.6 = (s32[4]{0:T(128)S(1)}, s32[4]{0:T(128)}, u32[]{:S(2)}) copy-start(s32[4]{0:T(128)} %param.25) | copy-start | bytes 52
  7.2 6.6 %copy-start.5 = (s32[4]{0:T(128)S(1)}, s32[4]{0:T(128)}, u32[]{:S(2)}) copy-start(s32[4]{0:T(128)} %param.24) | copy-start | bytes 52
  7.2 10.5 %copy-start = (bf16[2,128,2048]{2,1,0:T(8,128)(2,1)S(1)}, bf16[2,128,2048]{2,1,0:T(8,128)(2,1)}, u32[]{:S(2)}) copy-start(bf16[2,128,2048]{2,1,0:T(8,128)(2,1)} %param.22) | copy-start | bytes 3145732
  7.2 35.4 %copy-start.7 = (s32[2]{0:T(128)S(1)}, s32[2]{0:T(128)}, u32[]{:S(2)}) copy-start(s32[2]{0:T(128)} %param.23) | copy-start | bytes 28
  7.2 63.1 %all-reduce.4.cloned.1.call-start = ((), (), s32[]{:S(2)}) async-start(), calls=%async_computation.1 | async-start | bytes 786432 | tf_op jit(solution)/shard_map/psum | solution.py:111
  18.4 53.5 %all-to-all-start = ((bf16[4,16,2048]{2,1,0:T(8,128)(2,1)}), bf16[4,16,2048]{2,1,0:T(8,128)(2,1)S(1)}, u32[]{:S(2)}, u32[]{:S(2)}) async-start(bf16[4,16,2048]{2,1,0:T(8,128)(2,1)} %dynamic-slice_dynamic-update-slice_fusion), calls=%async_computation | async-start | bytes 524288 | tf_op jit(solution)/shard_map/all_to_all | solution.py:102
  23.5 83.8 %all-gather.5.cloned.1.call-start = ((), (), s32[]{:S(2)}) async-start(), calls=%async_computation.2 | async-start | bytes 1474560 | tf_op jit(solution)/shard_map/all_gather | solution.py:29
  71.9 6.0 %copy-start.1 = (bf16[1,16,2048]{2,1,0:T(8,128)(2,1)}, bf16[1,16,2048]{2,1,0:T(8,128)(2,1)S(1)}, u32[]{:S(2)}) copy-start(bf16[1,16,2048]{2,1,0:T(8,128)(2,1)S(1)} %constant_dynamic-slice_fusion.1) | copy-start | bytes 196612
  75.9 228.0 %all-reduce.6.cloned.1.call-start = ((), (), s32[]{:S(2)}) async-start(), calls=%async_computation.3 | async-start | bytes 1310720
  124.4 4.6 %collective-permute-start = (bf16[1,2,5,512]{3,2,1,0:T(8,128)(2,1)S(1)}, bf16[1,2,5,512]{3,2,1,0:T(8,128)(2,1)S(1)}, u32[]{:S(2)}, u32[]{:S(2)}) collective-permute-start(bf16[1,2,5,512]{3,2,1,0:T(8,128)(2,1)S(1)} %bitcast.160), channel_id=1, source_target_pairs={{0,31},{1,0},{2,1},{3,2},{4,3},{5,4},{6,5},{7,6},{8,7},{9,8},{10,9... | collective-permute-start | bytes 30728 | tf_op jit(solution)/shard_map/ppermute | solution.py:21
  128.9 4.0 %collective-permute-start.1 = (bf16[2,2,5,512]{3,2,1,0:T(8,128)(2,1)S(1)}, bf16[2,2,5,512]{3,2,1,0:T(8,128)(2,1)S(1)}, u32[]{:S(2)}, u32[]{:S(2)}) collective-permute-start(bf16[2,2,5,512]{3,2,1,0:T(8,128)(2,1)S(1)} %pad_maximum_fusion.3), channel_id=1, source_target_pairs={{0,30},{1,31},{2,0},{3,1},{4,2},{5,3},{6,4},{7,5},{8,6},{9,7},{10,... | collective-permute-start | bytes 61448 | tf_op jit(solution)/shard_map/ppermute | solution.py:21
  132.9 16.3 %copy-start.3 = (f32[4096]{0:T(1024)S(1)}, f32[4096]{0:T(1024)}, u32[]{:S(2)}) copy-start(f32[4096]{0:T(1024)} %param.18) | copy-start | bytes 49156
  132.9 5.2 %collective-permute-start.2 = (bf16[4,2,5,512]{3,2,1,0:T(8,128)(2,1)S(1)}, bf16[4,2,5,512]{3,2,1,0:T(8,128)(2,1)S(1)}, u32[]{:S(2)}, u32[]{:S(2)}) collective-permute-start(bf16[4,2,5,512]{3,2,1,0:T(8,128)(2,1)S(1)} %pad_maximum_fusion.2), channel_id=1, source_target_pairs={{0,28},{1,29},{2,30},{3,31},{4,0},{5,1},{6,2},{7,3},{8,4},{9,5},{1... | collective-permute-start | bytes 122888 | tf_op jit(solution)/shard_map/ppermute | solution.py:21
  138.2 6.2 %collective-permute-start.3 = (bf16[8,2,5,512]{3,2,1,0:T(8,128)(2,1)S(1)}, bf16[8,2,5,512]{3,2,1,0:T(8,128)(2,1)S(1)}, u32[]{:S(2)}, u32[]{:S(2)}) collective-permute-start(bf16[8,2,5,512]{3,2,1,0:T(8,128)(2,1)S(1)} %pad_maximum_fusion.1), channel_id=1, source_target_pairs={{0,24},{1,25},{2,26},{3,27},{4,28},{5,29},{6,30},{7,31},{8,0},{9,1... | collective-permute-start | bytes 245768 | tf_op jit(solution)/shard_map/ppermute | solution.py:21
  144.4 14.0 %collective-permute-start.4 = (bf16[16,2,5,512]{3,2,1,0:T(8,128)(2,1)S(1)}, bf16[16,2,5,512]{3,2,1,0:T(8,128)(2,1)S(1)}, u32[]{:S(2)}, u32[]{:S(2)}) collective-permute-start(bf16[16,2,5,512]{3,2,1,0:T(8,128)(2,1)S(1)} %get-tuple-element.255), channel_id=1, source_target_pairs={{0,16},{1,17},{2,18},{3,19},{4,20},{5,21},{6,22},{7,23},{8,24},{9,... | collective-permute-start | bytes 491528 | tf_op jit(solution)/shard_map/ppermute | solution.py:21
  159.6 3.5 %copy-start.4 = (bf16[4096,448]{0,1:T(8,128)(2,1)S(1)}, bf16[4096,448]{0,1:T(8,128)(2,1)}, u32[]{:S(2)}) copy-start(bf16[4096,448]{0,1:T(8,128)(2,1)} %param.20) | copy-start | bytes 11010052
Sparse Core Ops, SparseCore 0:
  12.0 58.2 all-reduce.3
  76.0 23.4 all-gather.4
  172.4 131.3 all-reduce.5
